TPU v7x, 32 devices: a whole 2x2x4 slice. The times are simulated.
32 devices in a mesh: wide: 8 (over y, x, core), narrow: 4 (over z).
Axes of the slice: x: 2, y: 2, z: 4, core: 2. Of those that a mesh axis runs over, the one named last changes fastest.
Arguments:
- embeds: bfloat16 [8192, 768], P(('wide', 'narrow')), may hold values from -6 to 6
- skip_tokens: bfloat16 [8192, 768], P(('wide', 'narrow')), may hold values from -6 to 6
- cotangent: bfloat16 [8192, 768], P(('wide', 'narrow')), may hold values from -6 to 6
- lengths: int32 [64], P(('wide', 'narrow')), may hold values from 32 to 128, as said below
- qkv_weight: float32 [2, 768, 2304], P(None, ('wide', 'narrow')), may hold values from -0.21875 to 0.21875
- out_weight: float32 [2, 768, 768], P(None, ('wide', 'narrow')), may hold values from -0.625 to 0.625
- up_weight: float32 [2, 768, 3072], P(None, ('wide', 'narrow')), may hold values from -0.21875 to 0.21875
- down_weight: float32 [2, 3072, 768], P(None, ('wide', 'narrow')), may hold values from -0.109375 to 0.109375
- up_bias: float32 [2, 3072], P(None, ('wide', 'narrow')), may hold values from -2 to 2
- norm_gains: float32 [2, 2, 768], P(None, None, ('wide', 'narrow')), may hold values from 0.5 to 1.5
- biases: float32 [2, 6, 768], P(None, None, ('wide', 'narrow')), may hold values from -2 to 2
- qkv_moments: float32 [2, 2, 768, 2304], P(None, None, ('wide', 'narrow')), as said below
- out_moments: float32 [2, 2, 768, 768], P(None, None, ('wide', 'narrow')), as said below
- up_moments: float32 [2, 2, 768, 3072], P(None, None, ('wide', 'narrow')), as said below
- down_moments: float32 [2, 2, 3072, 768], P(None, None, ('wide', 'narrow')), as said below
- up_bias_moments: float32 [2, 2, 3072], P(None, None, ('wide', 'narrow')), as said below
- gain_moments: float32 [2, 2, 2, 768], P(None, None, None, ('wide', 'narrow')), as said below
- bias_moments: float32 [2, 2, 6, 768], P(None, None, None, ('wide', 'narrow')), as said below
Outputs:
- head_output: bfloat16 [8192, 768], P(('wide', 'narrow'))
- embeds_grad: float32 [8192, 768], P(('wide', 'narrow'))
- skip_grad: float32 [8192, 768], P(('wide', 'narrow'))
- qkv_weight_step: float32 [2, 768, 2304], P(None, ('wide', 'narrow'))
- out_weight_step: float32 [2, 768, 768], P(None, ('wide', 'narrow'))
- up_weight_step: float32 [2, 768, 3072], P(None, ('wide', 'narrow'))
- down_weight_step: float32 [2, 3072, 768], P(None, ('wide', 'narrow'))
- up_bias_step: float32 [2, 3072], P(None, ('wide', 'narrow'))
- norm_gains_step: float32 [2, 2, 768], P(None, None, ('wide', 'narrow'))
- biases_step: float32 [2, 6, 768], P(None, None, ('wide', 'narrow'))
- qkv_moments_new: float32 [2, 2, 768, 2304], P(None, None, ('wide', 'narrow'))
- out_moments_new: float32 [2, 2, 768, 768], P(None, None, ('wide', 'narrow'))
- up_moments_new: float32 [2, 2, 768, 3072], P(None, None, ('wide', 'narrow'))
- down_moments_new: float32 [2, 2, 3072, 768], P(None, None, ('wide', 'narrow'))
- up_bias_moments_new: float32 [2, 2, 3072], P(None, None, ('wide', 'narrow'))
- gain_moments_new: float32 [2, 2, 2, 768], P(None, None, None, ('wide', 'narrow'))
- bias_moments_new: float32 [2, 2, 6, 768], P(None, None, None, ('wide', 'narrow'))
Inputs may be any that keep to these rules, and one draw needn't show every extreme that they name: `lengths`: positions at or past a span's length are padding; some span has length exactly 32 and some exactly 128. `qkv_moments`: index 0 of the first dimension holds first moments, index 1 second moments, which are positive. `out_moments`: index 0 of the first dimension holds first moments, index 1 second moments, which are positive. `up_moments`: index 0 of the first dimension holds first moments, index 1 second moments, which are positive. `down_moments`: index 0 of the first dimension holds first moments, index 1 second moments, which are positive. `up_bias_moments`: index 0 of the first dimension holds first moments, index 1 second moments, which are positive. `gain_moments`: index 0 of the first dimension holds first moments, index 1 second moments, which are positive. `bias_moments`: index 0 of the first dimension holds first moments, index 1 second moments, which are positive.
All inputs are finite; a program needn't handle non-finite values.
Results may differ from a plain program's by a relative error of at most 0.02.
Values may be sent and summed in bfloat16 or wider, within the bound.
A program may use at most 256 MiB of HBM per device.

v0:
```python
import jax
import jax.numpy as jnp
from jax import lax
from jax.sharding import PartitionSpec as P

HEADS = 12
SPAN = 128


norm_epsilon = 1e-12
score_scale = 0.125
masked_score = -1000000000.0
beta_first = 0.9
beta_second = 0.999
adam_epsilon = 1e-08
weight_decay = 0.01
first_fix = 1.0 - 0.9**10
second_fix = 1.0 - 0.999**10


def dot_first(left_side, right_side):
    return lax.dot_general(
        left_side, right_side, (((0,), (0,)), ((), ())), preferred_element_type=jnp.float32
    )


def dot_last(left_side, right_side):
    return lax.dot_general(
        left_side, right_side, (((1,), (1,)), ((), ())), preferred_element_type=jnp.float32
    )


def normalize(values, gain_row, shift_row):
    centred = values - jnp.mean(values, axis=-1, keepdims=True)
    inv_scale = lax.rsqrt(jnp.mean(centred * centred, axis=-1, keepdims=True) + norm_epsilon)
    normed = centred * inv_scale
    return (normed * gain_row + shift_row, normed, inv_scale)


def normalize_back(gradient, normed, inv_scale, gain_row):
    grad_gain = jnp.sum(gradient * normed, axis=0)
    grad_shift = jnp.sum(gradient, axis=0)
    scaled = gradient * gain_row
    grad_in = inv_scale * (
        scaled
        - jnp.mean(scaled, axis=-1, keepdims=True)
        - normed * jnp.mean(scaled * normed, axis=-1, keepdims=True)
    )
    return (grad_in, grad_gain, grad_shift)


def head_view(tensor):
    return tensor.reshape(tensor.shape[0] // SPAN, SPAN, HEADS, tensor.shape[1] // HEADS)


def attend_scores(queries, keys_low, key_valid):
    scores = (
        jnp.einsum(
            "bqhe,bkhe->bhqk",
            head_view(queries),
            head_view(keys_low),
            preferred_element_type=jnp.float32,
        )
        * score_scale
    )
    return jnp.where(key_valid[:, None, None, :], scores, masked_score)


def forward_block(weights, inputs, key_valid):
    qkv_w, out_w, up_w, down_w, up_b, gain_rows, biases = weights
    gains_wide = gain_rows.astype(jnp.float32)
    biases_wide = biases.astype(jnp.float32)
    row_count, model_width = inputs.shape
    mixed_in = jnp.dot(inputs, qkv_w, preferred_element_type=jnp.float32)
    queries = (mixed_in[:, :model_width] + biases_wide[0]).astype(jnp.bfloat16)
    keys_low = mixed_in[:, model_width : 2 * model_width].astype(jnp.bfloat16)
    values_low = (mixed_in[:, 2 * model_width :] + biases_wide[1]).astype(jnp.bfloat16)
    scores = attend_scores(queries, keys_low, key_valid)
    row_max = jnp.max(scores, axis=-1, keepdims=True)
    weights_exp = jnp.exp(scores - row_max)
    row_total = jnp.sum(weights_exp, axis=-1, keepdims=True)
    softmax_out = (weights_exp / row_total).astype(jnp.bfloat16)
    log_total = row_max + jnp.log(row_total)
    context = jnp.einsum(
        "bhqk,bkhe->bqhe", softmax_out, head_view(values_low), preferred_element_type=jnp.float32
    )
    context = context.reshape(row_count, model_width).astype(jnp.bfloat16)
    attended = jnp.dot(context, out_w, preferred_element_type=jnp.float32) + biases_wide[2]
    hidden, normed_one, scale_one = normalize(
        inputs.astype(jnp.float32) + attended, gains_wide[0], biases_wide[3]
    )
    hidden_low = hidden.astype(jnp.bfloat16)
    pre_gelu = jnp.dot(hidden_low, up_w, preferred_element_type=jnp.float32) + up_b.astype(
        jnp.float32
    )
    activated = jax.nn.gelu(pre_gelu, approximate=False).astype(jnp.bfloat16)
    branch_out = jnp.dot(activated, down_w, preferred_element_type=jnp.float32) + biases_wide[4]
    output, normed_two, scale_two = normalize(hidden + branch_out, gains_wide[1], biases_wide[5])
    saved = (
        queries,
        keys_low,
        values_low,
        log_total,
        context,
        normed_one,
        scale_one,
        hidden_low,
        pre_gelu,
        activated,
        normed_two,
        scale_two,
    )
    return (output, saved)


def backward_block(weights, inputs, key_valid, grad_out):
    qkv_w, out_w, up_w, down_w, up_b, gain_rows, biases = weights
    gains_wide = gain_rows.astype(jnp.float32)
    row_count, model_width = inputs.shape
    output, saved = forward_block(weights, inputs, key_valid)
    (
        queries,
        keys_low,
        values_low,
        log_total,
        context,
        normed_one,
        scale_one,
        hidden_low,
        pre_gelu,
        activated,
        normed_two,
        scale_two,
    ) = saved
    grad_pre_two, grad_gain_two, grad_shift_two = normalize_back(
        grad_out, normed_two, scale_two, gains_wide[1]
    )
    grad_branch = grad_pre_two.astype(jnp.bfloat16)
    grad_down_w = dot_first(activated, grad_branch)
    grad_act = dot_last(grad_branch, down_w)
    _, gelu_back = jax.vjp(lambda inner: jax.nn.gelu(inner, approximate=False), pre_gelu)
    grad_pre_gelu = gelu_back(grad_act)[0].astype(jnp.bfloat16)
    grad_up_w = dot_first(hidden_low, grad_pre_gelu)
    grad_hidden = grad_pre_two + dot_last(grad_pre_gelu, up_w)
    grad_pre_one, grad_gain_one, grad_shift_one = normalize_back(
        grad_hidden, normed_one, scale_one, gains_wide[0]
    )
    grad_attended = grad_pre_one.astype(jnp.bfloat16)
    grad_out_w = dot_first(context, grad_attended)
    grad_context = head_view(dot_last(grad_attended, out_w).astype(jnp.bfloat16))
    scores = attend_scores(queries, keys_low, key_valid)
    softmax_full = jnp.exp(scores - log_total)
    grad_probs = jnp.einsum(
        "bqhe,bkhe->bhqk", grad_context, head_view(values_low), preferred_element_type=jnp.float32
    )
    grad_values = jnp.einsum(
        "bhqk,bqhe->bkhe",
        softmax_full.astype(jnp.bfloat16),
        grad_context,
        preferred_element_type=jnp.float32,
    )
    grad_values = grad_values.reshape(row_count, model_width).astype(jnp.bfloat16)
    grad_scores = softmax_full * (
        grad_probs - jnp.sum(softmax_full * grad_probs, axis=-1, keepdims=True)
    )
    grad_scores = grad_scores.astype(jnp.bfloat16)
    grad_queries = (
        jnp.einsum(
            "bhqk,bkhe->bqhe", grad_scores, head_view(keys_low), preferred_element_type=jnp.float32
        )
        * score_scale
    )
    grad_queries = grad_queries.reshape(row_count, model_width).astype(jnp.bfloat16)
    grad_keys = (
        jnp.einsum(
            "bhqk,bqhe->bkhe", grad_scores, head_view(queries), preferred_element_type=jnp.float32
        )
        * score_scale
    )
    grad_keys = grad_keys.reshape(row_count, model_width).astype(jnp.bfloat16)
    grad_mixed = jnp.concatenate([grad_queries, grad_keys, grad_values], axis=1)
    grad_qkv_w = dot_first(inputs, grad_mixed)
    grad_inputs = grad_pre_one + dot_last(grad_mixed, qkv_w)
    grad_gains = jnp.stack([grad_gain_one, grad_gain_two])
    grad_biases = jnp.stack(
        [
            jnp.sum(grad_queries, axis=0, dtype=jnp.float32),
            jnp.sum(grad_values, axis=0, dtype=jnp.float32),
            jnp.sum(grad_attended, axis=0, dtype=jnp.float32),
            grad_shift_one,
            jnp.sum(grad_branch, axis=0, dtype=jnp.float32),
            grad_shift_two,
        ]
    )
    grads = (
        grad_qkv_w,
        grad_out_w,
        grad_up_w,
        grad_down_w,
        jnp.sum(grad_pre_gelu, axis=0, dtype=jnp.float32),
        grad_gains,
        grad_biases,
    )
    return (output, grad_inputs, grads)


def layer_pieces(params, layer_index):
    return tuple((parameter[layer_index].astype(jnp.bfloat16) for parameter in params))


def gather_forward(params, layer_index):
    pieces = layer_pieces(params, layer_index)
    return (
        lax.all_gather(pieces[0], ("wide", "narrow"), axis=0, tiled=True),
        lax.all_gather(pieces[1], ("wide", "narrow"), axis=0, tiled=True),
        lax.all_gather(pieces[2], ("wide", "narrow"), axis=0, tiled=True),
        lax.all_gather(pieces[3], ("wide", "narrow"), axis=0, tiled=True),
        lax.all_gather(pieces[4], ("wide", "narrow"), axis=0, tiled=True),
        lax.all_gather(pieces[5], ("wide", "narrow"), axis=1, tiled=True),
        lax.all_gather(pieces[6], ("wide", "narrow"), axis=1, tiled=True),
    )


def gather_backward(params, layer_index):
    pieces = layer_pieces(params, layer_index)
    return (
        lax.all_gather(pieces[0], ("wide", "narrow"), axis=0, tiled=True),
        lax.all_gather(pieces[1], ("wide", "narrow"), axis=0, tiled=True),
        lax.all_gather(pieces[2], ("wide", "narrow"), axis=0, tiled=True),
        lax.all_gather(pieces[3], ("wide", "narrow"), axis=0, tiled=True),
        lax.all_gather(pieces[4], ("wide", "narrow"), axis=0, tiled=True),
        lax.all_gather(pieces[5], ("wide", "narrow"), axis=1, tiled=True),
        lax.all_gather(pieces[6], ("wide", "narrow"), axis=1, tiled=True),
    )


def pack_owned(grads, owners):
    blocks = [grads[index].reshape(owners, -1) for index in range(5)]
    for index in (5, 6):
        tensor = grads[index]
        blocks.append(
            tensor.reshape(tensor.shape[0], owners, -1).transpose(1, 0, 2).reshape(owners, -1)
        )
    return jnp.concatenate(blocks, axis=1)


def unpack_owned(flat, local_shapes):
    pieces = []
    offset = 0
    for shape in local_shapes:
        count = 1
        for extent in shape:
            count = count * extent
        pieces.append(flat[offset : offset + count].reshape(shape))
        offset = offset + count
    return tuple(pieces)


def local_layer_shapes(params):
    return [parameter.shape[1:] for parameter in params]


def scatter_layer(grads, local_shapes):
    owners = lax.axis_size("wide") * lax.axis_size("narrow")
    packed = pack_owned(grads, owners)
    owned = lax.psum_scatter(packed, ("wide", "narrow"), scatter_dimension=0, tiled=True)
    return unpack_owned(owned.reshape(-1), local_shapes)


def adam_direction(parameter, moment, gradient, decayed):
    first_moment = beta_first * moment[0] + (1.0 - beta_first) * gradient
    second_moment = beta_second * moment[1] + (1.0 - beta_second) * gradient * gradient
    update = first_moment / first_fix / (jnp.sqrt(second_moment / second_fix) + adam_epsilon)
    update = update + decayed * weight_decay * parameter
    return (update, jnp.stack([first_moment, second_moment]))


def per_device(
    embeds,
    skip_tokens,
    cotangent,
    lengths,
    qkv_weight,
    out_weight,
    up_weight,
    down_weight,
    up_bias,
    norm_gains,
    biases,
    qkv_moments,
    out_moments,
    up_moments,
    down_moments,
    up_bias_moments,
    gain_moments,
    bias_moments,
):
    params = (qkv_weight, out_weight, up_weight, down_weight, up_bias, norm_gains, biases)
    moments = (
        qkv_moments,
        out_moments,
        up_moments,
        down_moments,
        up_bias_moments,
        gain_moments,
        bias_moments,
    )
    local_shapes = local_layer_shapes(params)
    span_count = lengths.shape[0]
    row_count, model_width = embeds.shape
    positions = lax.broadcasted_iota(jnp.int32, (span_count, SPAN), 1)
    key_valid = positions < lengths[:, None]
    row_index = lax.broadcasted_iota(jnp.int32, (1, SPAN, 1), 1)
    backbone_weights = gather_forward(params, 0)
    backbone_out, _ = forward_block(backbone_weights, embeds, key_valid)
    backbone_view = backbone_out.astype(jnp.bfloat16).reshape(span_count, SPAN, model_width)
    skip_view = skip_tokens.reshape(span_count, SPAN, model_width)
    head_in = jnp.where(row_index == 0, backbone_view, skip_view).reshape(row_count, model_width)
    head_weights = gather_forward(params, 1)
    head_out, grad_head_in, head_grads = backward_block(
        head_weights, head_in, key_valid, cotangent.astype(jnp.float32)
    )
    head_owned = scatter_layer(head_grads, local_shapes)
    grad_view = grad_head_in.reshape(span_count, SPAN, model_width)
    grad_backbone = jnp.where(row_index == 0, grad_view, 0.0).reshape(row_count, model_width)
    skip_grad = jnp.where(row_index == 0, 0.0, grad_view).reshape(row_count, model_width)
    backbone_again = gather_backward(params, 0)
    _, embeds_grad, backbone_grads = backward_block(
        backbone_again, embeds, key_valid, grad_backbone
    )
    backbone_owned = scatter_layer(backbone_grads, local_shapes)
    owned = tuple(
        (
            jnp.stack([first_part, second_part])
            for first_part, second_part in zip(backbone_owned, head_owned)
        )
    )
    new_steps = []
    new_moments = []
    for index in range(7):
        decayed = 1.0 if index < 4 else 0.0
        direction, moment = adam_direction(params[index], moments[index], owned[index], decayed)
        new_steps.append(direction)
        new_moments.append(moment)
    return (
        head_out.astype(jnp.bfloat16),
        embeds_grad,
        skip_grad,
        new_steps[0],
        new_steps[1],
        new_steps[2],
        new_steps[3],
        new_steps[4],
        new_steps[5],
        new_steps[6],
        new_moments[0],
        new_moments[1],
        new_moments[2],
        new_moments[3],
        new_moments[4],
        new_moments[5],
        new_moments[6],
    )


def solution(mesh):
    return jax.shard_map(
        per_device,
        mesh=mesh,
        in_specs=(
            P(("wide", "narrow"), None),
            P(("wide", "narrow"), None),
            P(("wide", "narrow"), None),
            P(("wide", "narrow")),
            P(None, ("wide", "narrow"), None),
            P(None, ("wide", "narrow"), None),
            P(None, ("wide", "narrow"), None),
            P(None, ("wide", "narrow"), None),
            P(None, ("wide", "narrow")),
            P(None, None, ("wide", "narrow")),
            P(None, None, ("wide", "narrow")),
            P(None, None, ("wide", "narrow"), None),
            P(None, None, ("wide", "narrow"), None),
            P(None, None, ("wide", "narrow"), None),
            P(None, None, ("wide", "narrow"), None),
            P(None, None, ("wide", "narrow")),
            P(None, None, None, ("wide", "narrow")),
            P(None, None, None, ("wide", "narrow")),
        ),
        out_specs=(
            P(("wide", "narrow"), None),
            P(("wide", "narrow"), None),
            P(("wide", "narrow"), None),
            P(None, ("wide", "narrow"), None),
            P(None, ("wide", "narrow"), None),
            P(None, ("wide", "narrow"), None),
            P(None, ("wide", "narrow"), None),
            P(None, ("wide", "narrow")),
            P(None, None, ("wide", "narrow")),
            P(None, None, ("wide", "narrow")),
            P(None, None, ("wide", "narrow"), None),
            P(None, None, ("wide", "narrow"), None),
            P(None, None, ("wide", "narrow"), None),
            P(None, None, ("wide", "narrow"), None),
            P(None, None, ("wide", "narrow")),
            P(None, None, None, ("wide", "narrow")),
            P(None, None, None, ("wide", "narrow")),
        ),
        check_vma=False,
    )
```

profile of v0, /device:TPU:9, one launch (start us, length us, event | category | flops | bytes accessed | tf_op | source)
XLA Modules:
  0.0 1587.9 jit_solution(7136878993017376273)
XLA Ops:
  16.3 62.5 %all-gather.8 = bf16[1,6,768]{1,0,2:T(2,128)(2,1)S(1)} all-gather(bf16[1,6,24]{1,0,2:T(2,128)(2,1)S(1)} %get-tuple-element.154), channel_id=10, replica_groups=mesh['wide'=8,'narrow'=4] {'wide','narrow'}, dimensions={2}, use_global_device_ids=true | all-gather | bytes 9504 | tf_op jit(solution)/shard_map/all_gather | solution.py:220
  79.3 13.4 slice_reduce_fusion
  93.2 47.8 %all-reduce.5 = (bf16[3072]{0:T(1024)(128)(2,1)S(1)}, bf16[3072]{0:T(1024)(128)(2,1)S(1)}) all-reduce(bf16[3072]{0:T(1024)(128)(2,1)S(1)} %dynamic-update-slice.1, bf16[3072]{0:T(1024)(128)(2,1)S(1)} %dynamic-update-slice), channel_id=14, replica_groups=mesh['wide'=8,'narrow'=4] {'wide','narrow'}, use_global_device_ids=true, to_apply=%add.1 | all-reduce | flops 6144 | bytes 24576
  141.6 62.3 %all-gather.1 = bf16[1,6,768]{1,0,2:T(2,128)(2,1)S(1)} all-gather(bf16[1,6,24]{1,0,2:T(2,128)(2,1)S(1)} %get-tuple-element.155), channel_id=3, replica_groups=mesh['wide'=8,'narrow'=4] {'wide','narrow'}, dimensions={2}, use_global_device_ids=true | all-gather | bytes 9504 | tf_op jit(solution)/shard_map/all_gather | solution.py:220
  204.4 13.4 slice_reduce_fusion.8
  218.6 71.5 %all-gather.3 = bf16[1,2,768]{1,0,2:T(2,128)(2,1)S(1)} all-gather(bf16[1,2,24]{1,0,2:T(2,128)(2,1)S(1)} %get-tuple-element.153), channel_id=5, replica_groups=mesh['wide'=8,'narrow'=4] {'wide','narrow'}, dimensions={2}, use_global_device_ids=true | all-gather | bytes 3168 | tf_op jit(solution)/shard_map/all_gather | solution.py:219
  290.5 5.1 slice_reduce_fusion.9
  296.2 69.0 %all-gather.10 = bf16[1,2,768]{1,0,2:T(2,128)(2,1)S(1)} all-gather(bf16[1,2,24]{1,0,2:T(2,128)(2,1)S(1)} %get-tuple-element.152), channel_id=12, replica_groups=mesh['wide'=8,'narrow'=4] {'wide','narrow'}, dimensions={2}, use_global_device_ids=true | all-gather | bytes 3168 | tf_op jit(solution)/shard_map/all_gather | solution.py:219
  365.6 5.1 slice_reduce_fusion.1
  370.7 3.1 fusion.28
  377.8 2.0 fusion.221
  380.1 11.8 multiply_convert_fusion.1
  392.0 4.5 fusion.222
  397.7 3.1 fusion.24
  410.6 2.0 fusion.224
  414.8 34.2 %all-gather.35.cloned.1.call-done = bf16[1,768,3072]{2,1,0:T(8,128)(2,1)} async-done(((bf16[1,24,3072]{2,1,0:T(8,128)(2,1)}), bf16[1,768,3072]{2,1,0:T(8,128)(2,1)}) %all-gather.35.cloned.1.call-update) | async-done | bytes 4718608 | tf_op jit(solution)/shard_map/all_gather | solution.py:216
  449.0 12.2 multiply_convert_fusion
  461.2 53.6 %all-gather.37.cloned.1.call-done = bf16[1,3072,768]{2,1,0:T(8,128)(2,1)} async-done(((bf16[1,96,768]{2,1,0:T(8,128)(2,1)}), bf16[1,3072,768]{2,1,0:T(8,128)(2,1)}) %all-gather.37.cloned.1.call-update) | async-done | bytes 4718608 | tf_op jit(solution)/shard_map/all_gather | solution.py:217
  514.8 4.6 fusion.225
  522.5 2.6 convert_reduce_fusion
  525.2 2.2 multiply_reduce_fusion.2
  530.5 1.9 copy.191
  532.4 1.9 reshape.1004
  541.0 2.0 multiply_reduce_fusion.3
  543.1 2.0 convert_reduce_fusion.7
  546.0 2.6 convert_reduce_fusion.1
  548.8 2.2 multiply_reduce_fusion.4
  553.1 1.9 copy.203
  555.0 1.8 reshape.1005
  562.1 1.9 fusion.133
  564.1 5.3 fusion.203
  569.4 5.1 fusion.192
  574.5 4.0 fusion.226
  578.5 1.9 fusion.130
  580.6 5.3 fusion.200
  585.9 5.1 fusion.197
  593.4 3.9 convolution_bitcast_fusion
  597.4 8.1 copy.215
  605.4 6.6 reshape.1006
  612.0 6.4 constant_dynamic-update-slice_fusion.9
  620.2 8.1 reshape.1008
  628.4 8.1 reshape.1009
  637.6 6.6 reshape.1013
  644.2 6.3 constant_dynamic-update-slice_fusion.19
  650.6 2.8 reshape.1014
  653.4 8.1 reshape.1015
  661.5 8.3 reshape.1016
  672.6 9.6 constant_dynamic-update-slice_fusion.7
  682.3 4.4 constant_dynamic-update-slice_fusion.6
  686.7 3.4 constant_dynamic-update-slice_fusion.18
  690.1 4.9 constant_dynamic-update-slice_fusion.17
  695.0 4.2 constant_dynamic-update-slice_fusion.16
  709.3 4.0 fusion.50
  713.3 799.2 %all-reduce.8.cloned.1.call-done = (f32[32,221472]{1,0:T(8,128)}, f32[32,221472]{1,0:T(8,128)}) async-done(((f32[32,221472]{1,0:T(8,128)}, f32[32,221472]{1,0:T(8,128)}), (f32[32,221472]{1,0:T(8,128)}, f32[32,221472]{1,0:T(8,128)})) %all-reduce.8.cloned.1.call-update) | async-done | bytes 56696848
  1517.3 2.0 dynamic-slice.5
  1519.2 3.7 fusion.212
  1522.9 3.7 fusion.211
  1532.2 2.0 fusion.207
  1534.2 2.0 fusion.206
  1545.2 2.1 fusion.126
  1548.0 2.1 multiply_add_fusion.4
  1558.4 2.3 fusion.110
  1563.5 2.3 fusion.116
  1573.1 2.1 pad_maximum_fusion.2
  (553 shorter events, 113.5 us)
Async XLA Ops:
  7.2 9.0 copy-start.87
  7.2 363.5 %all-gather.23.cloned.1.call-start = ((), (), s32[]{:S(2)}) async-start(), calls=%async_computation | async-start | bytes 3649536 | tf_op jit(solution)/shard_map/all_gather | solution.py:214
  9.1 368.7 %all-gather.25.cloned.1.call-start = ((), (), s32[]{:S(2)}) async-start(), calls=%async_computation.1 | async-start | bytes 1216512 | tf_op jit(solution)/shard_map/all_gather | solution.py:215
  10.7 369.4 %all-gather.27.cloned.1.call-start = ((), (), s32[]{:S(2)}) async-start(), calls=%async_computation.2 | async-start | bytes 4866048 | tf_op jit(solution)/shard_map/all_gather | solution.py:216
  11.9 80.8 %copy-start.127 = (f32[2,96]{1,0:T(2,128)S(1)}, f32[2,96]{1,0:T(2,128)}, u32[]{:S(2)}) copy-start(f32[2,96]{1,0:T(2,128)} %param.26) | copy-start | bytes 2308
  12.6 379.3 %all-gather.29.cloned.1.call-start = ((), (), s32[]{:S(2)}) async-start(), calls=%async_computation.3 | async-start | bytes 4866048 | tf_op jit(solution)/shard_map/all_gather | solution.py:217
  13.5 384.2 %all-gather.31.cloned.1.call-start = ((), (), s32[]{:S(2)}) async-start(), calls=%async_computation.4 | async-start | bytes 3649536 | tf_op jit(solution)/shard_map/all_gather | solution.py:214
  14.1 396.5 %all-gather.33.cloned.1.call-start = ((), (), s32[]{:S(2)}) async-start(), calls=%async_computation.5 | async-start | bytes 1216512 | tf_op jit(solution)/shard_map/all_gather | solution.py:215
  14.6 434.4 %all-gather.35.cloned.1.call-start = ((), (), s32[]{:S(2)}) async-start(), calls=%async_computation.6 | async-start | bytes 4866048 | tf_op jit(solution)/shard_map/all_gather | solution.py:216
  15.4 499.4 %all-gather.37.cloned.1.call-start = ((), (), s32[]{:S(2)}) async-start(), calls=%async_computation.7 | async-start | bytes 4866048 | tf_op jit(solution)/shard_map/all_gather | solution.py:217
  16.1 1496.4 %all-reduce.8.cloned.1.call-start = ((), (), s32[]{:S(2)}) async-start(), calls=%async_computation.8 | async-start | bytes 113442816
  79.2 139.2 %copy-start.129 = (s32[2]{0:T(128)S(1)}, s32[2]{0:T(128)}, u32[]{:S(2)}) copy-start(s32[2]{0:T(128)} %param.21) | copy-start | bytes 28
  79.2 139.2 %copy-start.112 = (f32[2,2,24]{2,1,0:T(2,128)S(1)}, f32[2,2,24]{2,1,0:T(2,128)}, u32[]{:S(2)}) copy-start(f32[2,2,24]{2,1,0:T(2,128)} %param.27) | copy-start | bytes 1156
  204.3 166.4 %copy-start.35 = (bf16[256,768]{1,0:T(8,128)(2,1)S(1)}, bf16[256,768]{1,0:T(8,128)(2,1)}, u32[]{:S(2)}) copy-start(bf16[256,768]{1,0:T(8,128)(2,1)} %param.18) | copy-start | bytes 1179652
  218.5 157.1 %copy-start.130 = (pred[2,128]{1,0:T(4,128)(4,1)}, pred[2,128]{1,0:T(4,128)(4,1)S(1)}, u32[]{:S(2)}) copy-start(pred[2,128]{1,0:T(4,128)(4,1)S(1)} %iota_compare_fusion) | copy-start | bytes 772
  377.7 14.2 copy-start.38
  379.8 12.1 copy-start.8
  379.8 12.1 copy-start.81
  380.0 11.9 copy-start.101
  380.1 11.8 copy-start.114
  514.8 7.6 slice-start.15
  514.8 7.6 slice-start.16
  514.8 7.6 copy-start.134
  551.8 10.3 copy-start.1
  628.3 8.2 copy-start.107
  628.3 8.2 copy-start.118
  628.3 8.3 copy-start.120
  628.3 8.6 copy-start.79
  628.3 8.6 copy-start.80
  628.3 8.7 copy-start.98
  628.3 8.8 copy-start.119
  628.3 8.9 copy-start.97
  628.3 9.0 copy-start.117
  661.5 8.4 copy-start.106
  661.5 8.5 copy-start.95
  661.5 8.6 copy-start.116
  661.5 8.8 copy-start.77
  661.5 8.9 copy-start.78
  661.5 9.0 copy-start.96
  661.5 9.0 copy-start.115
  661.5 9.1 copy-start.94
  661.5 9.2 copy-start.93
  671.0 11.2 slice-start
  672.6 9.7 slice-start.1
  672.6 9.7 slice-start.2
  672.6 17.5 %slice-start.6 = ((s8[9437184]{0:T(1024)(128)(4,1)}), s8[4194304]{0:T(1024)(128)(4,1)S(1)}, s32[]{:S(2)}) async-start(s8[9437184]{0:T(1024)(128)(4,1)} %bitcast.328), calls=%async_computation.15 | async-start | bytes 8388608
  672.6 17.5 %slice-start.7 = ((s8[9437184]{0:T(1024)(128)(4,1)}), s8[4194304]{0:T(1024)(128)(4,1)S(1)}, s32[]{:S(2)}) async-start(s8[9437184]{0:T(1024)(128)(4,1)} %bitcast.328), calls=%async_computation.16 | async-start | bytes 8388608
  682.3 7.8 slice-start.8
  686.7 8.3 slice-start.3
  713.3 829.8 %copy-start.88 = (f32[2,6,24]{2,0,1:T(2,128)S(1)}, f32[2,6,24]{2,0,1:T(2,128)}, u32[]{:S(2)}) copy-start(f32[2,6,24]{2,0,1:T(2,128)} %param.28) | copy-start | bytes 3460
  1515.8 29.4 %copy-start.16 = (f32[2,2,24,2304]{3,2,1,0:T(8,128)S(1)}, f32[2,2,24,2304]{3,2,1,0:T(8,128)}, u32[]{:S(2)}) copy-start(f32[2,2,24,2304]{3,2,1,0:T(8,128)} %param.29) | copy-start | bytes 2654212
  1515.8 29.4 %copy-start.34 = (f32[2,24,2304]{2,1,0:T(8,128)S(1)}, f32[2,24,2304]{2,1,0:T(8,128)}, u32[]{:S(2)}) copy-start(f32[2,24,2304]{2,1,0:T(8,128)} %param.22) | copy-start | bytes 1327108
  1517.2 26.5 %copy-start.59 = (f32[1,18432]{1,0:T(1,128)}, f32[1,18432]{1,0:T(1,128)S(1)}, u32[]{:S(2)}) copy-start(f32[1,18432]{1,0:T(1,128)S(1)} %dynamic-slice.4) | copy-start | bytes 221188
  1544.5 9.1 copy-start.58
  1548.0 10.4 copy-start.13
  1550.1 8.3 copy-start.27
  1565.8 11.1 copy-start.30
  1565.8 11.1 copy-start.31
  1573.0 6.1 copy-start.113
  1573.0 6.1 copy-start.121
  1573.0 6.1 copy-start.122
  1573.1 6.1 copy-start.128
  1573.1 6.7 copy-start.123
  1573.1 6.7 copy-start.124
  (97 other events, 296.5 us)
Sparse Core Ops, SparseCore 0:
  11.4 61.9 all-gather.22
  76.8 52.4 all-gather.24
  132.7 64.6 all-gather.26
  200.6 63.2 all-gather.28
  267.1 59.5 all-gather.30
  330.0 51.8 all-gather.32
  385.2 63.7 all-gather.34
  452.4 62.3 all-gather.36
  708.0 804.5 all-reduce.7
where the time goes:
time: 1600 us; the launch traced here: 1590 us
  waiting for transfers between devices  890 us (56%)
  blocking collectives  313 us (20%)
  local copies, waits for them, and re-layouts  222 us (14%)
  matrix products  107 us (7%)
  other arithmetic  40.3 us (3%)
  between operations  16.4 us (1%)
    unnamed x10, waiting for transfers between devices  802 us
    all_gather x2, blocking collectives, gather_forward(): lax.all_gather(pieces[5], ('wide', 'narrow'), axis=1, tiled=True)  140 us
    all_gather x2, blocking collectives, gather_forward(): lax.all_gather(pieces[6], ('wide', 'narrow'), axis=1, tiled=True)  125 us
    unnamed x351, local copies, waits for them, and re-layouts  62.7 us
    all_gather x2, waiting for transfers between devices, gather_forward(): lax.all_gather(pieces[3], ('wide', 'narrow'), axis=0, tiled=True)  53.6 us
    reshape x10, local copies, waits for them, and re-layouts, pack_owned(): blocks = [grads[index].reshape(owners, -1) for index in range(5)]  50.5 us
    unnamed x1, blocking collectives  47.8 us
    all_gather x2, waiting for transfers between devices, gather_forward(): lax.all_gather(pieces[2], ('wide', 'narrow'), axis=0, tiled=True)  34.2 us
  transfers between devices with their start and end apart: 9, of which 3 were waited for; matrix products, arithmetic and copies ran while one was open for 6% of the time, Pallas kernels for 0%

commit v1 on v0

--- a/solution.py
+++ b/solution.py
@@ -1,11 +1,12 @@
 import jax
 import jax.numpy as jnp
 from jax import lax
+from jax.experimental import pallas as pl
+from jax.experimental.pallas import tpu as pltpu
 from jax.sharding import PartitionSpec as P
 
 HEADS = 12
 SPAN = 128
-
 
 norm_epsilon = 1e-12
 score_scale = 0.125
@@ -204,68 +205,318 @@
     return (output, grad_inputs, grads)
 
 
-def layer_pieces(params, layer_index):
-    return tuple((parameter[layer_index].astype(jnp.bfloat16) for parameter in params))
-
-
-def gather_forward(params, layer_index):
-    pieces = layer_pieces(params, layer_index)
-    return (
-        lax.all_gather(pieces[0], ("wide", "narrow"), axis=0, tiled=True),
-        lax.all_gather(pieces[1], ("wide", "narrow"), axis=0, tiled=True),
-        lax.all_gather(pieces[2], ("wide", "narrow"), axis=0, tiled=True),
-        lax.all_gather(pieces[3], ("wide", "narrow"), axis=0, tiled=True),
-        lax.all_gather(pieces[4], ("wide", "narrow"), axis=0, tiled=True),
-        lax.all_gather(pieces[5], ("wide", "narrow"), axis=1, tiled=True),
-        lax.all_gather(pieces[6], ("wide", "narrow"), axis=1, tiled=True),
-    )
-
-
-def gather_backward(params, layer_index):
-    pieces = layer_pieces(params, layer_index)
-    return (
-        lax.all_gather(pieces[0], ("wide", "narrow"), axis=0, tiled=True),
-        lax.all_gather(pieces[1], ("wide", "narrow"), axis=0, tiled=True),
-        lax.all_gather(pieces[2], ("wide", "narrow"), axis=0, tiled=True),
-        lax.all_gather(pieces[3], ("wide", "narrow"), axis=0, tiled=True),
-        lax.all_gather(pieces[4], ("wide", "narrow"), axis=0, tiled=True),
-        lax.all_gather(pieces[5], ("wide", "narrow"), axis=1, tiled=True),
-        lax.all_gather(pieces[6], ("wide", "narrow"), axis=1, tiled=True),
-    )
-
-
-def pack_owned(grads, owners):
-    blocks = [grads[index].reshape(owners, -1) for index in range(5)]
-    for index in (5, 6):
-        tensor = grads[index]
-        blocks.append(
-            tensor.reshape(tensor.shape[0], owners, -1).transpose(1, 0, 2).reshape(owners, -1)
+MESH = pl.DeviceIdType.MESH
+
+
+def place():
+    wide = lax.axis_index("wide")
+    z = lax.axis_index("narrow")
+    return wide // 4, (wide // 2) % 2, wide % 2, z
+
+
+def device(y, x, c, z):
+    return ((y * 2 + x) * 2 + c, z)
+
+
+def flat(y, x, c, z):
+    return ((y * 2 + x) * 2 + c) * 4 + z
+
+
+def near(z, k):
+    if k == 0:
+        return z
+    if k == 1:
+        return z + 1 - 2 * (z % 2)
+    if k == 2:
+        return (z + 2) % 4
+    return 3 - z
+
+
+def greet(y, x, c, z):
+    barrier = pltpu.get_barrier_semaphore()
+    for there in (device(y, 1 - x, c, z), device(1 - y, x, c, z), device(y, x, 1 - c, z)):
+        pl.semaphore_signal(barrier, inc=1, device_id=there, device_id_type=MESH)
+
+    @pl.when(z < 3)
+    def _():
+        pl.semaphore_signal(barrier, inc=1, device_id=device(y, x, c, z + 1), device_id_type=MESH)
+
+    @pl.when(z > 0)
+    def _():
+        pl.semaphore_signal(barrier, inc=1, device_id=device(y, x, c, z - 1), device_id_type=MESH)
+
+    pl.semaphore_wait(barrier, 4 + ((z + 1) // 2) % 2)
+
+
+def run_if(pred, action):
+    if pred is None:
+        action()
+    else:
+        pl.when(pred)(action)
+
+
+class Sender:
+    def __init__(self, send_sem):
+        self.send_sem = send_sem
+        self.count = 0
+        self.pending = []
+
+    def send(self, src, dst, recv, there, pred=None):
+        copy = pltpu.make_async_remote_copy(
+            src_ref=src,
+            dst_ref=dst,
+            send_sem=self.send_sem.at[self.count],
+            recv_sem=recv,
+            device_id=there,
+            device_id_type=MESH,
         )
-    return jnp.concatenate(blocks, axis=1)
-
-
-def unpack_owned(flat, local_shapes):
-    pieces = []
-    offset = 0
-    for shape in local_shapes:
-        count = 1
-        for extent in shape:
-            count = count * extent
-        pieces.append(flat[offset : offset + count].reshape(shape))
-        offset = offset + count
-    return tuple(pieces)
-
-
-def local_layer_shapes(params):
-    return [parameter.shape[1:] for parameter in params]
-
-
-def scatter_layer(grads, local_shapes):
-    owners = lax.axis_size("wide") * lax.axis_size("narrow")
-    packed = pack_owned(grads, owners)
-    owned = lax.psum_scatter(packed, ("wide", "narrow"), scatter_dimension=0, tiled=True)
-    return unpack_owned(owned.reshape(-1), local_shapes)
-
+        self.count += 1
+        run_if(pred, copy.start)
+        self.pending.append((pred, copy))
+
+    def local(self, src, dst):
+        copy = pltpu.make_async_copy(src, dst, self.send_sem.at[self.count])
+        self.count += 1
+        copy.start()
+        return copy
+
+    def drain(self):
+        for pred, copy in self.pending:
+            run_if(pred, copy.wait_send)
+        self.pending = []
+
+
+def arrived(dst, recv, me, pred=None):
+    def wait():
+        pltpu.make_async_remote_copy(
+            src_ref=dst, dst_ref=dst, send_sem=recv, recv_sem=recv, device_id=me, device_id_type=MESH
+        ).wait_recv()
+
+    run_if(pred, wait)
+
+
+def gather_steps(sender, subs, recv_sem, base=0):
+    y, x, c, z = place()
+    sib = device(y, x, 1 - c, z)
+    xn = device(y, 1 - x, c, z)
+    yn = device(1 - y, x, c, z)
+
+    def there(sub, stage):
+        return (xn if stage == 1 else yn) if sub[2] == "x" else (yn if stage == 1 else xn)
+
+    def unit(sub, far1, far2, zz, core):
+        fx, fy = (far1, far2) if sub[2] == "x" else (far2, far1)
+        return flat(1 - y if fy else y, 1 - x if fx else x, core, zz)
+
+    def push(i, sub, src, slab_at, target, pred=None):
+        sender.send(src, sub[1](slab_at), recv_sem.at[base + i, slab_at], target, pred)
+
+    mine = flat(y, x, c, z)
+    locals_ = []
+    for i, sub in enumerate(subs):
+        own = sub[0]
+        push(i, sub, own, mine, device(y, x, c, z + 1), z < 3)
+        push(i, sub, own, mine, device(y, x, c, z - 1), z > 0)
+        push(i, sub, own, mine, there(sub, 1))
+        push(i, sub, own, mine, there(sub, 2))
+        push(i, sub, own, mine, sib)
+        locals_.append(sender.local(own, sub[1](mine)))
+    yield
+
+    def from_z(dist):
+        for i, sub in enumerate(subs):
+            for up in (True, False):
+                zz = z - dist if up else z + dist
+                have = (z >= dist) if up else (z <= 3 - dist)
+                at = flat(y, x, c, zz)
+
+                @pl.when(have)
+                def _(i=i, sub=sub, up=up, at=at):
+                    arrived(sub[1](at), recv_sem.at[base + i, at], device(y, x, c, z))
+
+                if dist < 3:
+                    if up:
+                        push(i, sub, sub[1](at), at, device(y, x, c, z + 1), (z >= dist) & (z < 3))
+                    else:
+                        push(i, sub, sub[1](at), at, device(y, x, c, z - 1), (z <= 3 - dist) & (z > 0))
+                push(i, sub, sub[1](at), at, there(sub, 1), have)
+                push(i, sub, sub[1](at), at, there(sub, 2), have)
+                push(i, sub, sub[1](at), at, sib, have)
+
+    def from_first(k):
+        for i, sub in enumerate(subs):
+            at = unit(sub, True, False, near(z, k), c)
+            arrived(sub[1](at), recv_sem.at[base + i, at], device(y, x, c, z))
+            push(i, sub, sub[1](at), at, there(sub, 2))
+            push(i, sub, sub[1](at), at, sib)
+
+    def from_second(far, k):
+        for i, sub in enumerate(subs):
+            at = unit(sub, far, True, near(z, k), c)
+            arrived(sub[1](at), recv_sem.at[base + i, at], device(y, x, c, z))
+            push(i, sub, sub[1](at), at, sib)
+
+    from_z(1)
+    yield
+    from_first(0)
+    yield
+    from_z(2)
+    yield
+    from_first(1)
+    yield
+    from_z(3)
+    yield
+    from_first(2)
+    from_first(3)
+    yield
+    for far in (False, True):
+        for k in range(4):
+            from_second(far, k)
+            yield
+    for i, sub in enumerate(subs):
+        for a in range(2):
+            for b in range(2):
+                for k in range(4):
+                    at = unit(sub, a == 1, b == 1, near(z, k), 1 - c)
+                    arrived(sub[1](at), recv_sem.at[base + i, at], device(y, x, c, z))
+    for copy in locals_:
+        copy.wait()
+
+
+SENDS_PER_GATHER = 6 + 2 * 4 + 2 * 4 + 2 * 3 + 4 * 2 + 8
+
+def reduce_steps(sender, subs, recv_sem, base=0):
+    y, x, c, z = place()
+    me = device(y, x, c, z)
+    sib = device(y, x, 1 - c, z)
+    xn = device(y, 1 - x, c, z)
+    yn = device(1 - y, x, c, z)
+    targets = (0, 3, 1, 2)
+
+    def chip(sub, far1, far2):
+        fx, fy = (far1, far2) if sub["dim"] == "x" else (far2, far1)
+        return (1 - y if fy else y), (1 - x if fx else x)
+
+    def own(sub, far1, far2, zz, core):
+        cy, cx = chip(sub, far1, far2)
+        return sub["own"](flat(cy, cx, core, zz))
+
+    def sib_slot(sub, far1, far2, zz):
+        cy, cx = chip(sub, far1, far2)
+        return (cy * 2 + cx) * 4 + zz
+
+    def first_of(sub):
+        return xn if sub["dim"] == "x" else yn
+
+    def second_of(sub):
+        return yn if sub["dim"] == "x" else xn
+
+    def coord1(sub, far):
+        here = x if sub["dim"] == "x" else y
+        return 1 - here if far else here
+
+    kinds = ((False, True), (True, True), (True, False), (False, False))
+
+    def start_sib(zz):
+        for i, sub in enumerate(subs):
+            for far1, far2 in kinds:
+                slot = sib_slot(sub, far1, far2, zz)
+                sender.send(
+                    own(sub, far1, far2, zz, 1 - c),
+                    sub["sib"].at[slot],
+                    recv_sem.at[base + i, slot],
+                    sib,
+                )
+
+    def take(sub, i, kind, slot):
+        buf = sub[kind].at[slot]
+        at = {"sib": 0, "second": 16, "first": 24, "chain": 28}[kind] + slot
+        arrived(buf, recv_sem.at[base + i, at], me)
+        return buf
+
+    def add_into(sub, dst, parts):
+        total = dst[...].astype(jnp.float32)
+        for part in parts:
+            total = total + part[...].astype(jnp.float32)
+        dst[...] = total.astype(dst.dtype)
+
+    def step_a(zz):
+        for i, sub in enumerate(subs):
+            for far1 in (False, True):
+                acc = own(sub, far1, True, zz, c)
+                add_into(sub, acc, [take(sub, i, "sib", sib_slot(sub, far1, True, zz))])
+                slot = coord1(sub, far1) * 4 + zz
+                sender.send(acc, sub["second"].at[slot], recv_sem.at[base + i, 16 + slot], second_of(sub))
+
+    def step_b(zz):
+        for i, sub in enumerate(subs):
+            acc = own(sub, True, False, zz, c)
+            parts = [
+                take(sub, i, "sib", sib_slot(sub, True, False, zz)),
+                take(sub, i, "second", coord1(sub, True) * 4 + zz),
+            ]
+            add_into(sub, acc, parts)
+            sender.send(acc, sub["first"].at[zz], recv_sem.at[base + i, 24 + zz], first_of(sub))
+
+    def chain_send(sub, i, acc, zz, up, pred):
+        slot = zz if up else jnp.where(z - 1 == zz, 4, zz)
+        there = device(y, x, c, z + 1) if up else device(y, x, c, z - 1)
+        sender.send(acc, sub["chain"].at[slot], recv_sem.at[base + i, 28 + slot], there, pred)
+
+    def step_c(zz):
+        for i, sub in enumerate(subs):
+            acc = own(sub, False, False, zz, c)
+            parts = [
+                take(sub, i, "sib", sib_slot(sub, False, False, zz)),
+                take(sub, i, "second", coord1(sub, False) * 4 + zz),
+                take(sub, i, "first", zz),
+            ]
+            add_into(sub, acc, parts)
+            if zz > 0:
+                chain_send(sub, i, acc, zz, True, z == 0)
+            if zz < 3:
+                chain_send(sub, i, acc, zz, False, z == 3)
+
+    def step_d(zz):
+        for i, sub in enumerate(subs):
+            acc = own(sub, False, False, zz, c)
+            for up in (True, False):
+                pred = (z > 0) & (z < zz) if up else (z < 3) & (z > zz)
+
+                @pl.when(pred)
+                def _(i=i, sub=sub, acc=acc):
+                    add_into(sub, acc, [take(sub, i, "chain", zz)])
+
+                chain_send(sub, i, acc, zz, up, pred)
+
+    def step_f():
+        for i, sub in enumerate(subs):
+            total = own(sub, False, False, z, c)[...].astype(jnp.float32)
+            sub["out"][...] = total
+
+            @pl.when(z > 0)
+            def _(i=i, sub=sub):
+                sub["out"][...] += take(sub, i, "chain", z)[...].astype(jnp.float32)
+
+            @pl.when(z < 3)
+            def _(i=i, sub=sub):
+                sub["out"][...] += take(sub, i, "chain", 4)[...].astype(jnp.float32)
+
+    t0, t1, t2, t3 = targets
+    for zz in targets:
+        start_sib(zz)
+    yield
+    for action, zz in (
+        (step_a, t0), (step_a, t1), (step_b, t0), (step_a, t2), (step_b, t1), (step_c, t0), (step_a, t3),
+        (step_b, t2), (step_d, t0), (step_c, t1), (step_b, t3), (step_d, t1), (step_c, t2), (step_d, t2),
+        (step_c, t3), (step_d, t3),
+    ):
+        action(zz)
+        yield
+    step_f()
+
+
+SENDS_PER_REDUCE = 16 + 8 + 4 + 12 + 12
 
 def adam_direction(parameter, moment, gradient, decayed):
     first_moment = beta_first * moment[0] + (1.0 - beta_first) * gradient
@@ -275,66 +526,343 @@
     return (update, jnp.stack([first_moment, second_moment]))
 
 
+def first_forward(weights, inputs, key_valid):
+    qkv_w, out_w, up_w, down_w, up_b, gain_rows, biases = weights
+    row_count, width = inputs.shape
+    span_count = row_count // SPAN
+    first = inputs.reshape(span_count, SPAN, width)[:, 0]
+    mixed = jnp.dot(inputs, qkv_w[:, width:], preferred_element_type=jnp.float32)
+    keys = mixed[:, :width].astype(jnp.bfloat16).reshape(span_count, SPAN, HEADS, width // HEADS)
+    values = (mixed[:, width:] + biases[1]).astype(jnp.bfloat16)
+    values = values.reshape(span_count, SPAN, HEADS, width // HEADS)
+    queries = jnp.dot(first, qkv_w[:, :width], preferred_element_type=jnp.float32) + biases[0]
+    queries = queries.astype(jnp.bfloat16).reshape(span_count, HEADS, width // HEADS)
+    scores = (
+        jnp.einsum("bhe,bkhe->bhk", queries, keys, preferred_element_type=jnp.float32) * score_scale
+    )
+    scores = jnp.where(key_valid[:, None, :], scores, masked_score)
+    probs = jax.nn.softmax(scores, axis=-1)
+    context = jnp.einsum(
+        "bhk,bkhe->bhe", probs.astype(jnp.bfloat16), values, preferred_element_type=jnp.float32
+    )
+    context = context.reshape(span_count, width).astype(jnp.bfloat16)
+    attended = jnp.dot(context, out_w, preferred_element_type=jnp.float32) + biases[2]
+    hidden, normed_one, scale_one = normalize(
+        first.astype(jnp.float32) + attended, gain_rows[0], biases[3]
+    )
+    hidden_low = hidden.astype(jnp.bfloat16)
+    pre_gelu = jnp.dot(hidden_low, up_w, preferred_element_type=jnp.float32) + up_b
+    activated = jax.nn.gelu(pre_gelu, approximate=False).astype(jnp.bfloat16)
+    branch_out = jnp.dot(activated, down_w, preferred_element_type=jnp.float32) + biases[4]
+    output, normed_two, scale_two = normalize(hidden + branch_out, gain_rows[1], biases[5])
+    saved = (
+        first, queries, keys, values, probs, context, normed_one, scale_one, hidden_low, pre_gelu,
+        activated, normed_two, scale_two,
+    )
+    return output, saved
+
+
+def first_backward(weights, inputs, saved, grad_out):
+    qkv_w, out_w, up_w, down_w, up_b, gain_rows, biases = weights
+    (
+        first, queries, keys, values, probs, context, normed_one, scale_one, hidden_low, pre_gelu,
+        activated, normed_two, scale_two,
+    ) = saved
+    row_count, width = inputs.shape
+    span_count = row_count // SPAN
+    grad_pre_two, grad_gain_two, grad_shift_two = normalize_back(
+        grad_out, normed_two, scale_two, gain_rows[1]
+    )
+    grad_branch = grad_pre_two.astype(jnp.bfloat16)
+    grad_act = dot_last(grad_branch, down_w)
+    _, gelu_back = jax.vjp(lambda inner: jax.nn.gelu(inner, approximate=False), pre_gelu)
+    grad_pre_gelu = gelu_back(grad_act)[0].astype(jnp.bfloat16)
+    grad_hidden = grad_pre_two + dot_last(grad_pre_gelu, up_w)
+    grad_pre_one, grad_gain_one, grad_shift_one = normalize_back(
+        grad_hidden, normed_one, scale_one, gain_rows[0]
+    )
+    grad_attended = grad_pre_one.astype(jnp.bfloat16)
+    grad_context = dot_last(grad_attended, out_w).astype(jnp.bfloat16)
+    grad_context = grad_context.reshape(span_count, HEADS, width // HEADS)
+    grad_probs = jnp.einsum(
+        "bhe,bkhe->bhk", grad_context, values, preferred_element_type=jnp.float32
+    )
+    grad_values = jnp.einsum("bhk,bhe->bkhe", probs.astype(jnp.bfloat16), grad_context)
+    grad_values = grad_values.reshape(row_count, width).astype(jnp.bfloat16)
+    grad_scores = probs * (grad_probs - jnp.sum(probs * grad_probs, axis=-1, keepdims=True))
+    grad_scores = grad_scores.astype(jnp.bfloat16)
+    grad_queries = (
+        jnp.einsum("bhk,bkhe->bhe", grad_scores, keys, preferred_element_type=jnp.float32)
+        * score_scale
+    )
+    grad_queries = grad_queries.reshape(span_count, width).astype(jnp.bfloat16)
+    grad_keys = (
+        jnp.einsum("bhk,bhe->bkhe", grad_scores, queries, preferred_element_type=jnp.float32)
+        * score_scale
+    )
+    grad_keys = grad_keys.reshape(row_count, width).astype(jnp.bfloat16)
+    grad_kv = jnp.concatenate([grad_keys, grad_values], axis=1)
+    grad_kv_w = dot_first(inputs, grad_kv)
+    grad_inputs = dot_last(grad_kv, qkv_w[:, width:])
+    grad_first = grad_pre_one + dot_last(grad_queries, qkv_w[:, :width])
+    placed = jnp.pad(grad_first[:, None], ((0, 0), (0, SPAN - 1), (0, 0))).reshape(row_count, width)
+    grad_inputs = grad_inputs + placed
+    rows = jnp.concatenate(
+        [context, grad_attended, hidden_low, grad_pre_gelu, activated, grad_branch, first, grad_queries],
+        axis=1,
+    )
+
+    def total(values):
+        return jnp.sum(values, axis=0, dtype=jnp.float32)
+
+    small = (
+        total(grad_pre_gelu),
+        jnp.stack([grad_gain_one, grad_gain_two]),
+        jnp.stack(
+            [
+                total(grad_queries), total(grad_values), total(grad_attended), grad_shift_one,
+                total(grad_branch), grad_shift_two,
+            ]
+        ),
+    )
+    return grad_inputs, grad_kv_w, rows, small
+
+
+def first_weight_grads(rows, kv_owned, at):
+    width = rows.shape[1] // 16
+    wide = 4 * width
+    context, grad_attended = rows[:, :width], rows[:, width : 2 * width]
+    hidden_low = rows[:, 2 * width : 3 * width]
+    grad_pre_gelu = rows[:, 3 * width : 3 * width + wide]
+    activated = rows[:, 7 * width : 11 * width]
+    grad_branch = rows[:, 11 * width : 12 * width]
+    first = rows[:, 12 * width : 13 * width]
+    grad_queries = rows[:, 13 * width : 14 * width]
+    count = kv_owned.shape[0]
+    own = lambda values, many: lax.dynamic_slice_in_dim(values, at * many, many, 1)
+    return (
+        jnp.concatenate([dot_first(own(first, count), grad_queries), kv_owned], axis=1),
+        dot_first(own(context, count), grad_attended),
+        dot_first(own(hidden_low, count), grad_pre_gelu),
+        dot_first(own(activated, 4 * count), grad_branch),
+    )
+
+
+def pack_small(up_b, gains, biases, owners):
+    parts = [up_b.reshape(owners, -1)]
+    for tensor in (gains, biases):
+        parts.append(tensor.reshape(tensor.shape[0], owners, -1).transpose(1, 0, 2).reshape(owners, -1))
+    return jnp.concatenate(parts, axis=1)
+
+
+def unpack_small(packed, width):
+    owners = packed.shape[0]
+    share = width // owners
+    up_b = packed[:, : 4 * share].reshape(4 * width)
+    gains = packed[:, 4 * share : 6 * share].reshape(owners, 2, share).transpose(1, 0, 2)
+    biases = packed[:, 6 * share :].reshape(owners, 6, share).transpose(1, 0, 2)
+    return up_b, gains.reshape(2, width), biases.reshape(6, width)
+
+
+def gather_kernel(p1, p2, small, w1a, w1b, w2a, w2b, small_out, send_sem, recv_sem):
+    y, x, c, z = place()
+    greet(y, x, c, z)
+    sender = Sender(send_sem)
+    subs = [(small, lambda u: small_out.at[u], "x")]
+    half = p1.shape[2] // 2
+    mid = p2.shape[1] // 2
+    for layer, (w1, w2) in enumerate(((w1a, w2a), (w1b, w2b))):
+        subs += [
+            (p1.at[layer, :, :half], lambda u, w1=w1: w1.at[u, :, :half], "x"),
+            (p1.at[layer, :, half:], lambda u, w1=w1: w1.at[u, :, half:], "y"),
+            (p2.at[layer, :mid], lambda u, w2=w2: w2.at[u, :mid], "x"),
+            (p2.at[layer, mid:], lambda u, w2=w2: w2.at[u, mid:], "y"),
+        ]
+    for _ in gather_steps(sender, subs, recv_sem):
+        pass
+    sender.drain()
+
+
+def gather_weights(p1, p2, small):
+    many = 9
+    hbm = pl.BlockSpec(memory_space=pl.ANY)
+    out = lambda a, rows: jax.ShapeDtypeStruct((32,) + rows, a.dtype)
+    return pl.pallas_call(
+        gather_kernel,
+        out_shape=[out(p1, p1.shape[1:])] * 2 + [out(p2, p2.shape[1:])] * 2 + [out(small, small.shape)],
+        in_specs=[hbm] * 3,
+        out_specs=[hbm] * 5,
+        scratch_shapes=[
+            pltpu.SemaphoreType.DMA((many * SENDS_PER_GATHER,)),
+            pltpu.SemaphoreType.DMA((many, 32)),
+        ],
+        compiler_params=pltpu.CompilerParams(collective_id=1, has_side_effects=True),
+    )(p1, p2, small)
+
+
+def reduce_kernel(g1, g2, kv, small, rows, o1, o2, okv, osmall, orows, v1, v2, vkv, vsmall, *rest):
+    y, x, c, z = place()
+    bufs, (send_sem, recv_sem, gather_sem, load_sem) = rest[:-4], rest[-4:]
+    loads = [
+        pltpu.make_async_copy(src, dst, load_sem.at[k])
+        for k, (src, dst) in enumerate(((g1, v1), (g2, v2), (kv, vkv), (small, vsmall)))
+    ]
+    for load in loads:
+        load.start()
+    greet(y, x, c, z)
+    for load in loads:
+        load.wait()
+    sender = Sender(send_sem)
+    subs = []
+
+    def add(own, out, dim):
+        k = 4 * len(subs)
+        subs.append(
+            dict(own=own, sib=bufs[k], second=bufs[k + 1], first=bufs[k + 2], chain=bufs[k + 3], out=out, dim=dim)
+        )
+
+    half, mid, half_kv = v1.shape[2] // 2, v2.shape[1] // 2, vkv.shape[2] // 2
+    add(lambda u: vsmall.at[u], osmall, "x")
+    add(lambda u: vkv.at[u, :, :half_kv], okv.at[:, :half_kv], "x")
+    add(lambda u: vkv.at[u, :, half_kv:], okv.at[:, half_kv:], "y")
+    add(lambda u: v1.at[u, :, :half], o1.at[:, :half], "x")
+    add(lambda u: v1.at[u, :, half:], o1.at[:, half:], "y")
+    add(lambda u: v2.at[u, :mid], o2.at[:mid], "x")
+    add(lambda u: v2.at[u, mid:], o2.at[mid:], "y")
+    spread = gather_steps(sender, [(rows, lambda u: orows.at[u], "x")], gather_sem)
+    for _ in reduce_steps(sender, subs, recv_sem):
+        next(spread, None)
+    for _ in spread:
+        pass
+    sender.drain()
+
+
+def reduce_grads(g1, g2, kv, small, rows):
+    hbm = pl.BlockSpec(memory_space=pl.ANY)
+    vmem = pl.BlockSpec(memory_space=pltpu.VMEM)
+    half = lambda a: (a.shape[1], a.shape[2] // 2)
+    blocks = [(small.shape[1:], small.dtype)]
+    blocks += [(half(kv), kv.dtype)] * 2 + [(half(g1), g1.dtype)] * 2
+    blocks += [((g2.shape[1] // 2, g2.shape[2]), g2.dtype)] * 2
+    scratch = [pltpu.VMEM(a.shape, a.dtype) for a in (g1, g2, kv, small)]
+    for shape, dtype in blocks:
+        scratch += [pltpu.VMEM((many,) + shape, dtype) for many in (16, 8, 4, 5)]
+    return pl.pallas_call(
+        reduce_kernel,
+        out_shape=[jax.ShapeDtypeStruct(a.shape[1:], jnp.float32) for a in (g1, g2, kv, small)]
+        + [jax.ShapeDtypeStruct((32,) + rows.shape, rows.dtype)],
+        in_specs=[hbm] * 5,
+        out_specs=[vmem] * 4 + [hbm],
+        scratch_shapes=scratch
+        + [
+            pltpu.SemaphoreType.DMA((len(blocks) * SENDS_PER_REDUCE + SENDS_PER_GATHER,)),
+            pltpu.SemaphoreType.DMA((len(blocks), 33)),
+            pltpu.SemaphoreType.DMA((1, 32)),
+            pltpu.SemaphoreType.DMA((4,)),
+        ],
+        compiler_params=pltpu.CompilerParams(
+            collective_id=2, has_side_effects=True, vmem_limit_bytes=63 * 2**20
+        ),
+    )(g1, g2, kv, small, rows)
+
+
+def exchange_weights(p1, p2, small, fast):
+    if fast:
+        w1a, w1b, w2a, w2b, small_all = gather_weights(p1, p2, small)
+        return (w1a, w1b), (w2a, w2b), small_all
+    both = ("wide", "narrow")
+    w1 = lax.all_gather(p1, both, axis=0)
+    w2 = lax.all_gather(p2, both, axis=0)
+    return (w1[:, 0], w1[:, 1]), (w2[:, 0], w2[:, 1]), lax.all_gather(small, both, axis=0)
+
+
+def exchange_grads(g1, g2, kv, small, rows, fast):
+    if fast:
+        return reduce_grads(g1, g2, kv, small, rows)
+    both = ("wide", "narrow")
+    summed = [
+        lax.psum_scatter(a, both, scatter_dimension=0).astype(jnp.float32) for a in (g1, g2, kv, small)
+    ]
+    return summed + [lax.all_gather(rows, both, axis=0)]
+
+
 def per_device(
-    embeds,
-    skip_tokens,
-    cotangent,
-    lengths,
-    qkv_weight,
-    out_weight,
-    up_weight,
-    down_weight,
-    up_bias,
-    norm_gains,
-    biases,
-    qkv_moments,
-    out_moments,
-    up_moments,
-    down_moments,
-    up_bias_moments,
-    gain_moments,
-    bias_moments,
+    embeds, skip_tokens, cotangent, lengths, qkv_weight, out_weight, up_weight, down_weight, up_bias,
+    norm_gains, biases, qkv_moments, out_moments, up_moments, down_moments, up_bias_moments,
+    gain_moments, bias_moments,
 ):
     params = (qkv_weight, out_weight, up_weight, down_weight, up_bias, norm_gains, biases)
     moments = (
-        qkv_moments,
-        out_moments,
-        up_moments,
-        down_moments,
-        up_bias_moments,
-        gain_moments,
-        bias_moments,
-    )
-    local_shapes = local_layer_shapes(params)
+        qkv_moments, out_moments, up_moments, down_moments, up_bias_moments, gain_moments, bias_moments,
+    )
+    wide_size, narrow_size = lax.axis_size("wide"), lax.axis_size("narrow")
+    fast = (wide_size, narrow_size) == (8, 4)
+    owners = wide_size * narrow_size
+    at = lax.axis_index("wide") * narrow_size + lax.axis_index("narrow")
     span_count = lengths.shape[0]
-    row_count, model_width = embeds.shape
+    row_count, width = embeds.shape
     positions = lax.broadcasted_iota(jnp.int32, (span_count, SPAN), 1)
     key_valid = positions < lengths[:, None]
     row_index = lax.broadcasted_iota(jnp.int32, (1, SPAN, 1), 1)
-    backbone_weights = gather_forward(params, 0)
-    backbone_out, _ = forward_block(backbone_weights, embeds, key_valid)
-    backbone_view = backbone_out.astype(jnp.bfloat16).reshape(span_count, SPAN, model_width)
-    skip_view = skip_tokens.reshape(span_count, SPAN, model_width)
-    head_in = jnp.where(row_index == 0, backbone_view, skip_view).reshape(row_count, model_width)
-    head_weights = gather_forward(params, 1)
+
+    p1 = jnp.concatenate([qkv_weight, out_weight, up_weight], axis=2).astype(jnp.bfloat16)
+    p2 = down_weight.astype(jnp.bfloat16)
+    share = 12 * width // owners
+    tiles = -(-2 * share // 1024)
+    small_own = jnp.concatenate(
+        [up_bias, norm_gains.reshape(2, -1), biases.reshape(2, -1)], axis=1
+    ).reshape(-1)
+    small_own = jnp.pad(small_own, (0, tiles * 1024 - 2 * share)).reshape(tiles * 8, 128)
+    w1, w2, small_all = exchange_weights(p1, p2, small_own, fast)
+    small_all = small_all.reshape(owners, -1)[:, : 2 * share].astype(jnp.bfloat16).astype(jnp.float32)
+
+    def layer_weights(layer):
+        joined = w1[layer].reshape(width, -1)
+        return (
+            joined[:, : 3 * width], joined[:, 3 * width : 4 * width], joined[:, 4 * width :],
+            w2[layer].reshape(-1, width),
+        ) + unpack_small(small_all[:, layer * share : (layer + 1) * share], width)
+
+    backbone, head = layer_weights(0), layer_weights(1)
+    backbone_out, saved = first_forward(backbone, embeds, key_valid)
+    skip_view = skip_tokens.reshape(span_count, SPAN, width)
+    head_in = jnp.where(row_index == 0, backbone_out.astype(jnp.bfloat16)[:, None], skip_view)
+    head_in = head_in.reshape(row_count, width)
     head_out, grad_head_in, head_grads = backward_block(
-        head_weights, head_in, key_valid, cotangent.astype(jnp.float32)
-    )
-    head_owned = scatter_layer(head_grads, local_shapes)
-    grad_view = grad_head_in.reshape(span_count, SPAN, model_width)
-    grad_backbone = jnp.where(row_index == 0, grad_view, 0.0).reshape(row_count, model_width)
-    skip_grad = jnp.where(row_index == 0, 0.0, grad_view).reshape(row_count, model_width)
-    backbone_again = gather_backward(params, 0)
-    _, embeds_grad, backbone_grads = backward_block(
-        backbone_again, embeds, key_valid, grad_backbone
-    )
-    backbone_owned = scatter_layer(backbone_grads, local_shapes)
-    owned = tuple(
-        (
-            jnp.stack([first_part, second_part])
-            for first_part, second_part in zip(backbone_owned, head_owned)
-        )
-    )
+        head, head_in, key_valid, cotangent.astype(jnp.float32)
+    )
+    grad_view = grad_head_in.reshape(span_count, SPAN, width)
+    skip_grad = jnp.where(row_index == 0, 0.0, grad_view).reshape(row_count, width)
+    embeds_grad, grad_kv_w, rows, small_first = first_backward(
+        backbone, embeds, saved, grad_view[:, 0]
+    )
+    low = lambda a: a.astype(jnp.bfloat16)
+    g1 = jnp.concatenate([low(head_grads[0]), low(head_grads[1]), low(head_grads[2])], axis=1)
+    g1 = g1.reshape(owners, width // owners, -1)
+    g2 = low(head_grads[3]).reshape(owners, -1, width)
+    kv = low(grad_kv_w).reshape(owners, width // owners, -1)
+    small_grads = jnp.concatenate(
+        [pack_small(*small_first, owners), pack_small(*head_grads[4:], owners)], axis=1
+    )
+    small_grads = jnp.pad(small_grads, ((0, 0), (0, tiles * 1024 - 2 * share)))
+    small_grads = small_grads.reshape(owners, tiles * 8, 128)
+    rows_wide = jnp.pad(rows, ((0, 0), (0, 2 * width)))
+    own_g1, own_g2, own_kv, own_small, all_rows = exchange_grads(
+        g1, g2, kv, small_grads, rows_wide.reshape(16 * span_count // 2, -1), fast
+    )
+    all_rows = all_rows.reshape(owners * span_count, -1)
+    first_grads = first_weight_grads(all_rows, own_kv, at)
+    own_small = own_small.reshape(-1)[: 2 * share].reshape(2, share)
+    sixth = width // owners
+    owned = [
+        jnp.stack([first_grads[0], own_g1[:, : 3 * width]]),
+        jnp.stack([first_grads[1], own_g1[:, 3 * width : 4 * width]]),
+        jnp.stack([first_grads[2], own_g1[:, 4 * width :]]),
+        jnp.stack([first_grads[3], own_g2]),
+        own_small[:, : 4 * sixth],
+        own_small[:, 4 * sixth : 6 * sixth].reshape(2, 2, sixth),
+        own_small[:, 6 * sixth :].reshape(2, 6, sixth),
+    ]
     new_steps = []
     new_moments = []
     for index in range(7):
@@ -342,25 +870,7 @@
         direction, moment = adam_direction(params[index], moments[index], owned[index], decayed)
         new_steps.append(direction)
         new_moments.append(moment)
-    return (
-        head_out.astype(jnp.bfloat16),
-        embeds_grad,
-        skip_grad,
-        new_steps[0],
-        new_steps[1],
-        new_steps[2],
-        new_steps[3],
-        new_steps[4],
-        new_steps[5],
-        new_steps[6],
-        new_moments[0],
-        new_moments[1],
-        new_moments[2],
-        new_moments[3],
-        new_moments[4],
-        new_moments[5],
-        new_moments[6],
-    )
+    return (head_out.astype(jnp.bfloat16), embeds_grad, skip_grad, *new_steps, *new_moments)
 
 
 def solution(mesh):

time: 1600 us -> 408 us (0.26)
  the two profiles are of different devices: /device:TPU:9 before, /device:TPU:16 now
where the time goes in v1:
time: 408 us; the launch traced here: 401 us
  Pallas kernels  235 us (58%)
  matrix products  77.9 us (19%)
  other arithmetic  46.8 us (11%)
  local copies, waits for them, and re-layouts  38.2 us (9%)
    pallas_call x1, Pallas kernels, gather_weights(): pl.pallas_call(gather_kernel, out_shape=[out(p1, p1.shape[1:])] * 2 + [ou...  126 us
    pallas_call x1, Pallas kernels, reduce_grads(): pl.pallas_call(reduce_kernel, out_shape=[jax.ShapeDtypeStruct(a.shape[1:]...  109 us
    dot_general x9, matrix products, dot_last(): lax.dot_general(left_side, right_side, (((1,), (1,)), ((), ())), preferre...  23 us
    dot_general x9, matrix products, dot_first(): lax.dot_general(left_side, right_side, (((0,), (0,)), ((), ())), preferre...  15.5 us
    dot_general x1, matrix products, forward_block(): jnp.dot(hidden_low, up_w, preferred_element_type=jnp.float32)  11.7 us
    reduce_sum x4, other arithmetic, total(): return jnp.sum(values, axis=0, dtype=jnp.float32)  11.7 us

profile of v1, /device:TPU:16, one launch (start us, length us, event | category | flops | bytes accessed | tf_op | source)
XLA Modules:
  0.0 400.9 jit_solution(17169689645464076846)
XLA Ops:
  0.7 1.2 convert.27
  1.9 1.0 convert.25
  2.9 0.9 convert.26
  3.9 0.9 pad_maximum_fusion.4.p1
  4.7 0.7 convert_element_type.217.p2
  6.4 125.9 %shard_map.305 = (bf16[32,24,6144]{2,1,0:T(8,128)(2,1)}, bf16[32,24,6144]{2,1,0:T(8,128)(2,1)}, bf16[32,96,768]{2,1,0:T(8,128)(2,1)}, bf16[32,96,768]{2,1,0:T(8,128)(2,1)}, f32[32,8,128]{2,1,0:T(8,128)}) custom-call(bf16[2,24,6144]{2,1,0:T(8,128)(2,1)} %pad_maximum_fusion.4.p1, bf16[2,96,768]{2,1,0:T(8,128)(2,1)} %convert_element_type.217.p2, ...), custom_call_target="tpu_custom_call" | custom-call | tf_op jit(solution)/shard_map/pallas_call | solution.py:690
  132.3 0.9 convert.28
  133.6 1.5 fusion.58
  135.3 2.5 convolution_bitcast_fusion
  138.2 0.9 fusion.217
  140.8 1.7 fusion.218
  144.5 3.1 fusion.13
  147.7 3.3 fusion.219
  152.4 3.2 fusion.24
  156.8 0.9 copy.178
  157.7 1.8 reshape.855
  159.9 1.7 fusion.220
  163.8 1.9 fusion.221
  167.1 11.7 %multiply_convert_fusion = (bf16[256,3072]{1,0:T(8,128)(2,1)}, f32[256,3072]{1,0:T(8,128)}, f32[256,3072]{1,0:T(8,128)}) fusion(f32[3072]{0:T(1024)S(1)} %add.407, bf16[768,6144]{1,0:T(8,128)(2,1)} %bitcast.331, f32[256,768]{1,0:T(8,128)S(1)} %get-tuple-element.185, f32[768]{0:T(1024)S(1)} %add.404, f32[768]{0:T(1024)S(1)} %mul.795, ...), kind=kOutput, calls=%fused_computation.21 | convolution fusion | flops 1260847104 | bytes 13389824 | tf_op jit(solution)/shard_map/dot_general | solution.py:94
  179.6 4.4 %fusion.222 = (f32[256]{0:T(256)S(1)}, f32[256,768]{1,0:T(8,128)S(1)}) fusion(f32[768]{0:T(1024)} %add.410, bf16[256,3072]{1,0:T(8,128)(2,1)} %get-tuple-element.115, bf16[3072,768]{1,0:T(8,128)(2,1)} %bitcast.346, f32[768]{0:T(1024)S(1)} %add.404, f32[768]{0:T(1024)S(1)} %mul.795, f32[256]{0:T(256)} %copy-done.80, f32[256,768]{1,0:T(8,128)S(1)} %get-tuple-element.185, ...), kind=kOutput, calls=%fused_computation.410 | convolution fusion | flops 1209335552 | bytes 7876608 | tf_op jit(solution)/shard_map/dot_general | solution.py:98
  185.4 1.4 copy.190
  186.7 1.4 mul.804
  188.1 1.7 fusion.71
  190.4 1.4 copy.191
  191.8 1.4 add.415
  193.2 2.6 convert_reduce_fusion.2
  195.8 7.2 %convert_reduce_fusion = (f32[3072]{0:T(1024)}, bf16[256,3072]{1,0:T(8,128)(2,1)S(1)}) fusion(f32[256,3072]{1,0:T(8,128)} %get-tuple-element.116, f32[256,3072]{1,0:T(8,128)} %get-tuple-element.186, bf16[3072,768]{1,0:T(8,128)(2,1)} %bitcast.347, f32[256,768]{1,0:T(8,128)S(1)} %get-tuple-element.106), kind=kOutput, calls=%fused_computation.19 | convolution fusion | flops 1220736000 | bytes 13381632 | tf_op jit(solution)/shard_map/dot_general | solution.py:29
  203.1 2.2 multiply_reduce_fusion.1
  205.3 0.9 convert_reduce_fusion.3
  207.0 0.7 log_add_fusion
  207.7 1.3 convert_reduce_fusion.4
  212.7 4.6 %broadcast_select_fusion = (f32[256,768]{1,0:T(8,128)}, f32[256,768]{1,0:T(8,128)S(1)}) fusion(pred[256]{0:T(512)(128)(4,1)S(1)} %copy-done.104, f32[256,768]{1,0:T(8,128)S(1)} %get-tuple-element.108, bf16[256,2304]{0,1:T(8,128)(2,1)S(1)} %bitcast_dynamic-update-slice_fusion.2, bf16[768,6144]{1,0:T(8,128)(2,1)} %bitcast.332), kind=kOutput, calls=%fused_computation.189 | convolution fusion | flops 906362880 | bytes 7078144 | tf_op jit(solution)/shard_map/dot_general | solution.py:29
  217.7 1.5 convert_reduce_fusion.7
  219.4 1.5 multiply_reduce_fusion.7
  222.2 0.8 fusion.223
  225.5 11.6 %convert_reduce_fusion.6 = (f32[12,64]{1,0:T(8,128)S(1)}, bf16[2,12,64,128]{3,0,2,1:T(2,128)(2,1)}) fusion(bf16[2,12,128]{2,0,1:T(2,128)(2,1)S(1)} %copy.207, bf16[2,12,64]{0,2,1:T(8,128)(2,1)S(1)} %bitcast.319), kind=kLoop, calls=%fused_computation.120 | loop fusion | flops 589056 | bytes 405504 | tf_op jit(solution)/shard_map/reduce_sum | solution.py:616
  239.1 3.6 convolution_convert_fusion
  242.8 1.1 convolution_convert_fusion.2
  244.0 1.5 convolution_convert_fusion.4
  245.5 2.4 copy.209
  247.9 3.3 convolution_convert_fusion.1
  251.2 4.5 %pad_maximum_fusion = bf16[768,6144]{1,0:T(8,128)(2,1)} fusion(bf16[768,3072]{1,0:T(8,128)(2,1)S(1)} %convolution_convert_fusion.1, bf16[768,768]{1,0:T(8,128)(2,1)S(1)} %copy-done.3, bf16[768,2304]{1,0:T(8,128)(2,1)S(1)} %convolution_convert_fusion.2), kind=kLoop, calls=%fused_computation.2 | loop fusion | flops 28311552 | bytes 18874368 | tf_op jit(solution)/shard_map/concatenate | solution.py:840
  255.8 0.8 reshape.847
  257.3 1.0 bitcast_dynamic-update-slice_fusion
  258.3 0.9 copy-done.17
  259.2 3.3 convolution_convert_fusion.3
  262.5 109.3 %shard_map.306 = (f32[24,6144]{1,0:T(8,128)}, f32[96,768]{1,0:T(8,128)}, f32[24,1536]{1,0:T(8,128)}, f32[8,128]{1,0:T(8,128)}, bf16[32,16,1536]{2,1,0:T(8,128)(2,1)}) custom-call(bf16[32,24,6144]{2,1,0:T(8,128)(2,1)} %bitcast.286, bf16[32,96,768]{2,1,0:T(8,128)(2,1)} %bitcast.287, bf16[32,24,1536]{2,1,0:T(8,128)(2,1)} %bitcast.302, f32[32,8,128]{2,1,0:T(8,128)} %bitcast.323, ...), custom_call_target="tpu_custom_call" | custom-call | tf_op jit(solution)/shard_map/pallas_call | solution.py:750
  371.9 0.9 reshape.877
  375.9 2.7 reshape.875
  378.6 0.8 slice.343
  379.4 1.0 fusion.136
  380.7 1.1 pad_maximum_fusion.2
  382.4 1.0 fusion.105
  383.5 1.1 slice_bitcast_fusion
  384.6 1.5 multiply_add_fusion.2
  386.1 1.1 pad_maximum_fusion.1
  387.5 0.7 pad_maximum_fusion.11
  388.8 1.0 pad_maximum_fusion.3
  389.8 1.2 fusion.89
  391.0 1.2 fusion.83
  392.3 0.8 fusion.133
  393.1 1.1 fusion.99
  395.5 1.7 fusion.51
  397.3 3.4 fusion.30
  (433 shorter events, 31.8 us)
Async XLA Ops:
  0.7 4.1 %copy-start.12 = (f32[2,96,768]{2,1,0:T(8,128)S(1)}, f32[2,96,768]{2,1,0:T(8,128)}, u32[]{:S(2)}) copy-start(f32[2,96,768]{2,1,0:T(8,128)} %param.25) | copy-start | bytes 1769476
  0.7 4.8 %copy-start.68 = (f32[2,6,24]{2,0,1:T(2,128)S(1)}, f32[2,6,24]{2,0,1:T(2,128)}, u32[]{:S(2)}) copy-start(f32[2,6,24]{2,0,1:T(2,128)} %param.28) | copy-start | bytes 3460
  0.7 4.9 %copy-start.90 = (f32[2,2,24]{2,1,0:T(2,128)S(1)}, f32[2,2,24]{2,1,0:T(2,128)}, u32[]{:S(2)}) copy-start(f32[2,2,24]{2,1,0:T(2,128)} %param.27) | copy-start | bytes 1156
  0.7 4.9 %copy-start.94 = (f32[2,96]{1,0:T(2,128)S(1)}, f32[2,96]{1,0:T(2,128)}, u32[]{:S(2)}) copy-start(f32[2,96]{1,0:T(2,128)} %param.26) | copy-start | bytes 2308
  0.7 132.9 %copy-start.33 = (bf16[256,768]{1,0:T(8,128)(2,1)S(1)}, bf16[256,768]{1,0:T(8,128)(2,1)}, u32[]{:S(2)}) copy-start(bf16[256,768]{1,0:T(8,128)(2,1)} %param.18) | copy-start | bytes 1179652
  133.6 7.1 %copy-start.56 = (bf16[2,1,768]{2,1,0:T(2,128)(2,1)}, bf16[2,1,768]{2,1,0:T(2,128)(2,1)S(1)}, u32[]{:S(2)}) copy-start(bf16[2,1,768]{2,1,0:T(2,128)(2,1)S(1)} %slice.300) | copy-start | bytes 9220
  137.9 9.6 %copy-start.36 = (bf16[2,128,12,64]{1,0,3,2:T(2,128)(2,1)}, bf16[2,128,12,64]{1,0,3,2:T(2,128)(2,1)S(1)}, u32[]{:S(2)}) copy-start(bf16[2,128,12,64]{1,0,3,2:T(2,128)(2,1)S(1)} %reshape.848) | copy-start | bytes 1179652
  139.1 4.6 %copy-start.42 = (f32[2,12,128]{2,1,0:T(8,128)}, f32[2,12,128]{2,1,0:T(8,128)S(1)}, u32[]{:S(2)}) copy-start(f32[2,12,128]{2,1,0:T(8,128)S(1)} %get-tuple-element.177) | copy-start | bytes 36868
  140.2 7.4 %copy-start.38 = (bf16[2,128,12,64]{1,0,3,2:T(2,128)(2,1)}, bf16[2,128,12,64]{1,0,3,2:T(2,128)(2,1)S(1)}, u32[]{:S(2)}) copy-start(bf16[2,128,12,64]{1,0,3,2:T(2,128)(2,1)S(1)} %reshape.849) | copy-start | bytes 1179652
  143.7 7.4 %copy-start.47 = (f32[2,768]{1,0:T(2,128)}, f32[2,768]{1,0:T(2,128)S(1)}, u32[]{:S(2)}) copy-start(f32[2,768]{1,0:T(2,128)S(1)} %get-tuple-element.120) | copy-start | bytes 18436
  147.6 4.9 %copy-start.34 = (f32[2,3072]{1,0:T(2,128)}, f32[2,3072]{1,0:T(2,128)S(1)}, u32[]{:S(2)}) copy-start(f32[2,3072]{1,0:T(2,128)S(1)} %fusion.13) | copy-start | bytes 73732
  147.6 4.7 %copy-start.40 = (bf16[256,768]{1,0:T(8,128)(2,1)S(1)}, bf16[256,768]{1,0:T(8,128)(2,1)}, u32[]{:S(2)}) copy-start(bf16[256,768]{1,0:T(8,128)(2,1)} %param.19) | copy-start | bytes 1179652
  152.4 11.4 %copy-start.10 = (bf16[256,768]{1,0:T(8,128)(2,1)}, bf16[256,768]{1,0:T(8,128)(2,1)S(1)}, u32[]{:S(2)}) copy-start(bf16[256,768]{1,0:T(8,128)(2,1)S(1)} %bitcast_select_fusion) | copy-start | bytes 1179652
  163.6 15.2 %copy-start.21 = (bf16[2,128,12,64]{1,0,3,2:T(2,128)(2,1)}, bf16[2,128,12,64]{1,0,3,2:T(2,128)(2,1)S(1)}, u32[]{:S(2)}) copy-start(bf16[2,128,12,64]{1,0,3,2:T(2,128)(2,1)S(1)} %copy.184) | copy-start | bytes 1179652
  165.7 39.6 %copy-start = (f32[256,768]{1,0:T(8,128)}, f32[256,768]{1,0:T(8,128)S(1)}, u32[]{:S(2)}) copy-start(f32[256,768]{1,0:T(8,128)S(1)} %get-tuple-element.185) | copy-start | bytes 2359300
  165.7 13.1 %copy-start.65 = (f32[256]{0:T(256)}, f32[256]{0:T(256)S(1)}, u32[]{:S(2)}) copy-start(f32[256]{0:T(256)S(1)} %broadcast_multiply_fusion.6) | copy-start | bytes 3076
  166.0 12.9 %copy-start.80 = (f32[256]{0:T(256)}, f32[256]{0:T(256)S(1)}, u32[]{:S(2)}) copy-start(f32[256]{0:T(256)S(1)} %add_rsqrt_fusion.1) | copy-start | bytes 3076
  167.1 11.8 %copy-start.53 = (f32[1,32,24]{1,2,0:T(8,128)S(1)}, f32[1,32,24]{1,2,0:T(8,128)}, u32[]{:S(2)}) copy-start(f32[1,32,24]{1,2,0:T(8,128)} %get-tuple-element.152) | copy-start | bytes 9220
  179.6 8.5 %copy-start.20 = (bf16[256,768]{1,0:T(8,128)(2,1)S(1)}, bf16[256,768]{1,0:T(8,128)(2,1)}, u32[]{:S(2)}) copy-start(bf16[256,768]{1,0:T(8,128)(2,1)} %param.20) | copy-start | bytes 1179652
  193.2 9.8 %slice-start.5 = ((s8[9437184]{0:T(1024)(128)(4,1)}), s8[4194304]{0:T(1024)(128)(4,1)S(1)}, s32[]{:S(2)}) async-start(s8[9437184]{0:T(1024)(128)(4,1)} %bitcast.333), calls=%async_computation.5 | async-start | bytes 8388608
  195.8 7.2 %copy-start.8 = (f32[256,768]{1,0:T(8,128)}, f32[256,768]{1,0:T(8,128)S(1)}, u32[]{:S(2)}) copy-start(f32[256,768]{1,0:T(8,128)S(1)} %get-tuple-element.106) | copy-start | bytes 2359300
  195.8 7.2 %slice-start.6 = ((s8[9437184]{0:T(1024)(128)(4,1)}), s8[4194304]{0:T(1024)(128)(4,1)S(1)}, s32[]{:S(2)}) async-start(s8[9437184]{0:T(1024)(128)(4,1)} %bitcast.333), calls=%async_computation.6 | async-start | bytes 8388608
  195.8 7.2 %slice-start.7 = ((s8[9437184]{0:T(1024)(128)(4,1)}), s8[1048576]{0:T(1024)(128)(4,1)S(1)}, s32[]{:S(2)}) async-start(s8[9437184]{0:T(1024)(128)(4,1)} %bitcast.333), calls=%async_computation.7 | async-start | bytes 2097152
  195.8 7.2 %copy-start.66 = (f32[256]{0:T(256)S(1)}, f32[256]{0:T(256)}, u32[]{:S(2)}) copy-start(f32[256]{0:T(256)} %copy-done.65) | copy-start | bytes 3076
  195.8 7.2 %copy-start.81 = (f32[256]{0:T(256)S(1)}, f32[256]{0:T(256)}, u32[]{:S(2)}) copy-start(f32[256]{0:T(256)} %copy-done.80) | copy-start | bytes 3076
  206.2 6.5 %copy-start.1 = (f32[256,768]{1,0:T(8,128)}, f32[256,768]{1,0:T(8,128)S(1)}, u32[]{:S(2)}) copy-start(f32[256,768]{1,0:T(8,128)S(1)} %get-tuple-element.108) | copy-start | bytes 2359300
  209.5 9.8 %slice-start.2 = ((s8[9437184]{0:T(1024)(128)(4,1)}), s8[4194304]{0:T(1024)(128)(4,1)S(1)}, s32[]{:S(2)}) async-start(s8[9437184]{0:T(1024)(128)(4,1)} %bitcast.298), calls=%async_computation.2 | async-start | bytes 8388608
  210.5 8.8 %slice-start.3 = ((s8[9437184]{0:T(1024)(128)(4,1)}), s8[4194304]{0:T(1024)(128)(4,1)S(1)}, s32[]{:S(2)}) async-start(s8[9437184]{0:T(1024)(128)(4,1)} %bitcast.298), calls=%async_computation.3 | async-start | bytes 8388608
  212.4 5.2 %slice-start = ((s8[4718592]{0:T(1024)(128)(4,1)}), s8[4194304]{0:T(1024)(128)(4,1)S(1)}, s32[]{:S(2)}) async-start(s8[4718592]{0:T(1024)(128)(4,1)} %bitcast.289), calls=%async_computation | async-start | bytes 8388608
  212.7 4.7 %copy-start.15 = (bf16[256,2304]{0,1:T(8,128)(2,1)}, bf16[256,2304]{0,1:T(8,128)(2,1)S(1)}, u32[]{:S(2)}) copy-start(bf16[256,2304]{0,1:T(8,128)(2,1)S(1)} %bitcast_dynamic-update-slice_fusion.2) | copy-start | bytes 3538948
  212.7 4.7 %copy-start.52 = (f32[2,768]{1,0:T(2,128)S(1)}, f32[2,768]{1,0:T(2,128)}, u32[]{:S(2)}) copy-start(f32[2,768]{1,0:T(2,128)} %get-tuple-element.118) | copy-start | bytes 18436
  212.7 4.9 %copy-start.97 = (f32[2]{0:T(128)S(1)}, f32[2]{0:T(128)}, u32[]{:S(2)}) copy-start(f32[2]{0:T(128)} %copy-done.96) | copy-start | bytes 28
  212.7 5.0 %slice-start.1 = ((s8[4718592]{0:T(1024)(128)(4,1)}), s8[524288]{0:T(1024)(128)(4,1)S(1)}, s32[]{:S(2)}) async-start(s8[4718592]{0:T(1024)(128)(4,1)} %bitcast.289), calls=%async_computation.1 | async-start | bytes 1048576
  212.7 5.0 %copy-start.35 = (f32[2,3072]{1,0:T(2,128)S(1)}, f32[2,3072]{1,0:T(2,128)}, u32[]{:S(2)}) copy-start(f32[2,3072]{1,0:T(2,128)} %copy-done.34) | copy-start | bytes 73732
  212.7 6.6 %slice-start.4 = ((s8[9437184]{0:T(1024)(128)(4,1)}), s8[1048576]{0:T(1024)(128)(4,1)S(1)}, s32[]{:S(2)}) async-start(s8[9437184]{0:T(1024)(128)(4,1)} %bitcast.298), calls=%async_computation.4 | async-start | bytes 2097152
  219.4 4.7 %copy-start.58 = (f32[12,64]{1,0:T(8,128)S(1)}, f32[12,64]{1,0:T(8,128)}, u32[]{:S(2)}) copy-start(f32[12,64]{1,0:T(8,128)} %get-tuple-element.203) | copy-start | bytes 9220
  219.4 4.9 %copy-start.76 = (f32[768]{0:T(1024)S(1)}, f32[768]{0:T(1024)}, u32[]{:S(2)}) copy-start(f32[768]{0:T(1024)} %get-tuple-element.107) | copy-start | bytes 9220
  219.4 5.0 %copy-start.93 = (f32[768]{0:T(1024)S(1)}, f32[768]{0:T(1024)}, u32[]{:S(2)}) copy-start(f32[768]{0:T(1024)} %get-tuple-element.93) | copy-start | bytes 9220
  219.4 5.1 %copy-start.75 = (f32[768]{0:T(1024)S(1)}, f32[768]{0:T(1024)}, u32[]{:S(2)}) copy-start(f32[768]{0:T(1024)} %get-tuple-element.105) | copy-start | bytes 9220
  219.4 5.2 %copy-start.74 = (f32[768]{0:T(1024)S(1)}, f32[768]{0:T(1024)}, u32[]{:S(2)}) copy-start(f32[768]{0:T(1024)} %get-tuple-element.95) | copy-start | bytes 9220
  219.4 5.4 %copy-start.92 = (f32[768]{0:T(1024)S(1)}, f32[768]{0:T(1024)}, u32[]{:S(2)}) copy-start(f32[768]{0:T(1024)} %get-tuple-element.88) | copy-start | bytes 9220
  219.4 5.5 %copy-start.73 = (f32[768]{0:T(1024)S(1)}, f32[768]{0:T(1024)}, u32[]{:S(2)}) copy-start(f32[768]{0:T(1024)} %get-tuple-element.90) | copy-start | bytes 9220
  220.9 17.3 %copy-start.83 = (f32[3072]{0:T(1024)S(1)}, f32[3072]{0:T(1024)}, u32[]{:S(2)}) copy-start(f32[3072]{0:T(1024)} %get-tuple-element.199) | copy-start | bytes 36868
  220.9 18.2 %copy-start.6 = (bf16[256,3072]{1,0:T(8,128)(2,1)S(1)}, bf16[256,3072]{1,0:T(8,128)(2,1)}, u32[]{:S(2)}) copy-start(bf16[256,3072]{1,0:T(8,128)(2,1)} %get-tuple-element.115) | copy-start | bytes 4718596
  220.9 18.2 %copy-start.9 = (f32[256,768]{1,0:T(8,128)S(1)}, f32[256,768]{1,0:T(8,128)}, u32[]{:S(2)}) copy-start(f32[256,768]{1,0:T(8,128)} %copy-done.8) | copy-start | bytes 2359300
  221.1 21.7 %copy-start.45 = (f32[2,768]{1,0:T(2,128)}, f32[2,768]{1,0:T(2,128)S(1)}, u32[]{:S(2)}) copy-start(f32[2,768]{1,0:T(2,128)S(1)} %get-tuple-element.104) | copy-start | bytes 18436
  244.0 3.9 copy-start.67
  244.0 3.9 copy-start.82
  251.2 5.3 %copy-start.79 = (f32[2,12,128]{2,1,0:T(8,128)S(1)}, f32[2,12,128]{2,1,0:T(8,128)}, u32[]{:S(2)}) copy-start(f32[2,12,128]{2,1,0:T(8,128)} %get-tuple-element.193) | copy-start | bytes 36868
  262.5 110.4 %copy-start.84 = (f32[2,2,6,24]{3,1,2,0:T(2,128)S(1)}, f32[2,2,6,24]{3,1,2,0:T(2,128)}, u32[]{:S(2)}) copy-start(f32[2,2,6,24]{3,1,2,0:T(2,128)} %param.35) | copy-start | bytes 6916
  262.5 111.6 %copy-start.77 = (f32[2,2,2,24]{3,2,1,0:T(2,128)S(1)}, f32[2,2,2,24]{3,2,1,0:T(2,128)}, u32[]{:S(2)}) copy-start(f32[2,2,2,24]{3,2,1,0:T(2,128)} %param.34) | copy-start | bytes 2308
  262.5 112.2 %copy-start.95 = (f32[2,96]{1,0:T(2,128)S(1)}, f32[2,96]{1,0:T(2,128)}, u32[]{:S(2)}) copy-start(f32[2,96]{1,0:T(2,128)} %param.26) | copy-start | bytes 2308
  262.5 112.3 %copy-start.98 = (f32[2,2,96]{2,1,0:T(2,128)S(1)}, f32[2,2,96]{2,1,0:T(2,128)}, u32[]{:S(2)}) copy-start(f32[2,2,96]{2,1,0:T(2,128)} %param.33) | copy-start | bytes 4612
  371.8 8.6 %copy-start.4 = (f32[2,2,96,768]{3,2,1,0:T(8,128)S(1)}, f32[2,2,96,768]{3,2,1,0:T(8,128)}, u32[]{:S(2)}) copy-start(f32[2,2,96,768]{3,2,1,0:T(8,128)} %param.32) | copy-start | bytes 3538948
  371.9 8.6 %copy-start.29 = (f32[96,768]{1,0:T(8,128)S(1)}, f32[96,768]{1,0:T(8,128)}, u32[]{:S(2)}) copy-start(f32[96,768]{1,0:T(8,128)} %get-tuple-element.35) | copy-start | bytes 884740
  374.1 6.6 %copy-start.88 = (f32[2,48]{1,0:T(2,128)}, f32[2,48]{1,0:T(2,128)S(1)}, u32[]{:S(2)}) copy-start(f32[2,48]{1,0:T(2,128)S(1)} %slice.346) | copy-start | bytes 1156
  383.5 3.9 copy-start.31
  383.5 3.9 copy-start.30
  384.6 3.9 copy-start.44
  391.0 3.9 copy-start.78
  391.0 3.9 copy-start.91
  391.0 4.5 %copy-start.46 = (f32[2,768]{1,0:T(2,128)S(1)}, f32[2,768]{1,0:T(2,128)}, u32[]{:S(2)}) copy-start(f32[2,768]{1,0:T(2,128)} %copy-done.45) | copy-start | bytes 18436
  391.0 4.5 %copy-start.62 = (bf16[2,768]{1,0:T(2,128)(2,1)S(1)}, bf16[2,768]{1,0:T(2,128)(2,1)}, u32[]{:S(2)}) copy-start(bf16[2,768]{1,0:T(2,128)(2,1)} %copy-done.61) | copy-start | bytes 9220
  392.3 5.1 %copy-start.18 = (bf16[256,1536]{0,1:T(8,128)(2,1)S(1)}, bf16[256,1536]{0,1:T(8,128)(2,1)}, u32[]{:S(2)}) copy-start(bf16[256,1536]{0,1:T(8,128)(2,1)} %copy-done.17) | copy-start | bytes 2359300
  (50 other events, 107.5 us)
